TPU v7x, 512 devices: a whole 4x4x16 slice. The times are simulated.
512 devices in a mesh: grp: 16 (over z_hi, x), seq: 32 (over y, z_lo, core).
Axes of the slice: x: 4, y: 4, z: 16 (z_hi: 4, z_lo: 4; z = z_hi * 4 + z_lo), core: 2. Of those that a mesh axis runs over, the one named last changes fastest.
Arguments:
- queries: bfloat16 [262144, 384], P(('grp', 'seq')), may hold values from -6 to 6
- keys: bfloat16 [262144, 384], P(('grp', 'seq')), may hold values from -6 to 6
- values: bfloat16 [262144, 384], P(('grp', 'seq')), may hold values from -6 to 6
- offsets: int32 [2, 6], replicated, may hold values from 0 to 127, as said below
- out_weight: bfloat16 [384, 768], replicated, may hold values from -1.1953125 to 1.1953125
Outputs:
- mixed: bfloat16 [262144, 768], P(('grp', 'seq'))
Inputs may be any that keep to these rules, and one draw needn't show every extreme that they name: Row 0 holds offsets below 8, row 1 offsets below 128; in each row one head has offset 0 and another the row's largest allowed value.
All inputs are finite; a program needn't handle non-finite values.
Results may differ from a plain program's by a relative error of at most 0.0052.
Values may be sent and summed in bfloat16 or wider, within the bound.
A program may use at most 64 MiB of HBM per device.

v0:
```python
import math

import jax
import jax.numpy as jnp
from jax import lax
from jax.sharding import PartitionSpec as P

HEAD_DIM = 64
KEEP = 2048


NEGATIVE = -1e30


def pick_rows(source, dilation, shifts):
    lanes = jnp.arange(dilation, dtype=jnp.int32)
    chosen = jnp.repeat(lanes[:, None] == shifts[None, :], HEAD_DIM, axis=1)
    grouped = source.reshape(source.shape[0] // dilation, dilation, source.shape[1])
    return jnp.sum(jnp.where(chosen[None], grouped, jnp.zeros((), source.dtype)), axis=1)


def spread_rows(source, dilation, shifts, filler, repeat_by):
    lanes = jnp.arange(dilation, dtype=jnp.int32)
    chosen = jnp.repeat(lanes[:, None] == shifts[None, :], repeat_by, axis=1)
    spread = jnp.where(chosen[None], source[:, None, :], filler)
    return spread.reshape(source.shape[0] * dilation, source.shape[1])


def attend(asks, keys_in, values_in):
    count_ask = asks.shape[0]
    count_key = keys_in.shape[0]
    head_count = asks.shape[1] // HEAD_DIM
    asks_h = asks.reshape(count_ask, head_count, HEAD_DIM)
    keys_h = keys_in.reshape(count_key, head_count, HEAD_DIM)
    values_h = values_in.reshape(count_key, head_count, HEAD_DIM)
    scores = jnp.einsum("qhe,khe->hqk", asks_h, keys_h, preferred_element_type=jnp.float32) * (
        1.0 / math.sqrt(HEAD_DIM)
    )
    allowed = (
        jnp.arange(count_key, dtype=jnp.int32)[None, :]
        <= jnp.arange(count_ask, dtype=jnp.int32)[:, None]
    )
    scores = jnp.where(allowed[None], scores, NEGATIVE)
    highest = jnp.max(scores, axis=-1)
    weights = jnp.where(allowed[None], jnp.exp(scores - highest[..., None]), 0.0)
    totals = jnp.sum(weights, axis=-1)
    summed = jnp.einsum(
        "hqk,khe->qhe", weights.astype(jnp.bfloat16), values_h, preferred_element_type=jnp.float32
    )
    output = (summed / totals.T[:, :, None]).reshape(count_ask, head_count * HEAD_DIM)
    return (output, (highest + jnp.log(totals)).T)


def empty_state(count_ask, head_count):
    return (
        jnp.full((head_count, count_ask), NEGATIVE, jnp.float32),
        jnp.zeros((head_count, count_ask), jnp.float32),
        jnp.zeros((count_ask, head_count * HEAD_DIM), jnp.float32),
    )


def fold_piece(carry, piece, asks, first):
    highest, totals, accum = carry
    count_key = piece[0].shape[0]
    count_ask = asks.shape[0]
    head_count = highest.shape[0]
    keys_h = piece[0].reshape(count_key, head_count, HEAD_DIM)
    values_h = piece[1].reshape(count_key, head_count, HEAD_DIM)
    asks_h = asks.reshape(count_ask, head_count, HEAD_DIM)
    scores = jnp.einsum("qhe,khe->hqk", asks_h, keys_h, preferred_element_type=jnp.float32) * (
        1.0 / math.sqrt(HEAD_DIM)
    )
    allowed = (
        jnp.arange(count_key, dtype=jnp.int32)[None, :]
        <= (first + jnp.arange(count_ask, dtype=jnp.int32))[:, None]
    )
    scores = jnp.where(allowed[None], scores, NEGATIVE)
    newest = jnp.maximum(highest, jnp.max(scores, axis=-1))
    weights = jnp.where(allowed[None], jnp.exp(scores - newest[..., None]), 0.0)
    factor = jnp.exp(highest - newest)
    totals = jnp.sum(weights, axis=-1)
    added = jnp.einsum(
        "hqk,khe->qhe", weights.astype(jnp.bfloat16), values_h, preferred_element_type=jnp.float32
    )
    accum = accum * jnp.repeat(factor.T, HEAD_DIM, axis=1) + added.reshape(
        count_ask, head_count * HEAD_DIM
    )
    return (newest, totals, accum)


def finish_state(carry):
    highest, totals, accum = carry
    output = accum / jnp.repeat(totals.T, HEAD_DIM, axis=1)
    return (output, (highest + jnp.log(totals)).T)


def merge_levels(outputs, spreads):
    highest = jnp.maximum(jnp.maximum(spreads[0], spreads[1]), spreads[2])
    shares = [jnp.exp(item - highest) for item in spreads]
    numer = jnp.repeat(shares[0], HEAD_DIM, axis=1) * outputs[0]
    numer = numer + jnp.repeat(shares[1], HEAD_DIM, axis=1) * outputs[1]
    numer = numer + jnp.repeat(shares[2], HEAD_DIM, axis=1) * outputs[2]
    denom = shares[0] + shares[1] + shares[2]
    return (numer / jnp.repeat(denom, HEAD_DIM, axis=1)).astype(jnp.bfloat16)


def on_device(queries, keys, values, offsets, out_weight):
    row_count = queries.shape[0]
    head_count = queries.shape[1] // HEAD_DIM
    seq_count = lax.axis_size("seq")
    grp_count = lax.axis_size("grp")
    device_count = seq_count * grp_count
    near_rate = row_count * seq_count // KEEP
    far_rate = row_count * device_count // KEEP
    near_shift = offsets[0]
    far_shift = offsets[1]
    near_q = pick_rows(queries, near_rate, near_shift)
    near_k = pick_rows(keys, near_rate, near_shift)
    near_v = pick_rows(values, near_rate, near_shift)
    far_q = pick_rows(queries, far_rate, far_shift)
    far_k = pick_rows(keys, far_rate, far_shift)
    far_v = pick_rows(values, far_rate, far_shift)
    near_first = lax.axis_index("seq") * near_q.shape[0]
    far_first = (lax.axis_index("grp") * seq_count + lax.axis_index("seq")) * far_q.shape[0]
    near_init = empty_state(near_q.shape[0], head_count)
    far_init = empty_state(far_q.shape[0], head_count)
    near_state = fold_piece(
        near_init,
        (
            lax.all_gather(near_k, "seq", axis=0, tiled=True),
            lax.all_gather(near_v, "seq", axis=0, tiled=True),
        ),
        near_q,
        near_first,
    )
    far_state = fold_piece(
        far_init,
        (
            lax.all_gather(far_k, ("grp", "seq"), axis=0, tiled=True),
            lax.all_gather(far_v, ("grp", "seq"), axis=0, tiled=True),
        ),
        far_q,
        far_first,
    )
    near_out, near_lse = finish_state(near_state)
    far_out, far_lse = finish_state(far_state)
    block_out, block_lse = attend(queries, keys, values)
    outputs = [
        block_out,
        spread_rows(near_out, near_rate, near_shift, 0.0, HEAD_DIM),
        spread_rows(far_out, far_rate, far_shift, 0.0, HEAD_DIM),
    ]
    spreads = [
        block_lse,
        spread_rows(near_lse, near_rate, near_shift, NEGATIVE, 1),
        spread_rows(far_lse, far_rate, far_shift, NEGATIVE, 1),
    ]
    merged = merge_levels(outputs, spreads)
    return jnp.dot(merged, out_weight, preferred_element_type=jnp.float32).astype(jnp.bfloat16)


def solution(mesh):
    placed = (P(("grp", "seq"), None), P(("grp", "seq"), None), P(("grp", "seq"), None), P(), P())
    return jax.shard_map(
        on_device, mesh=mesh, in_specs=placed, out_specs=P(("grp", "seq"), None), check_vma=False
    )
```

profile of v0, /device:TPU:1, one launch (start us, length us, event | category | flops | bytes accessed | tf_op | source)
XLA Modules:
  0.0 1682.2 jit_solution(14708311136743086879)
XLA Ops:
  6.5 0.8 slice_bitcast_fusion.1
  7.7 2.6 fusion.56
  11.1 1.2 copy.54
  12.4 1.2 copy.63
  14.0 2.1 select_reduce_fusion.1
  18.3 0.9 reshape.244
  19.4 1.2 fusion
  20.6 1.5 fusion.2
  22.2 1.1 copy-done.1
  23.4 57.6 %all-gather.9.cloned.1.call-done = bf16[2048,384]{1,0:T(8,128)(2,1)} async-done(((bf16[64,384]{1,0:T(8,128)(2,1)}), bf16[2048,384]{1,0:T(8,128)(2,1)}) %all-gather.9.cloned.1.call-update) | async-done | bytes 1572880 | tf_op jit(solution)/shard_map/all_gather | solution.py:131
  81.0 2.7 copy.60
  83.7 63.3 %all-gather.7.cloned.1.call-done = bf16[2048,384]{1,0:T(8,128)(2,1)} async-done(((bf16[64,384]{1,0:T(8,128)(2,1)}), bf16[2048,384]{1,0:T(8,128)(2,1)}) %all-gather.7.cloned.1.call-update) | async-done | bytes 1572880 | tf_op jit(solution)/shard_map/all_gather | solution.py:130
  147.0 1.7 copy.50
  148.7 0.8 fusion.76
  149.5 0.8 fusion.11
  150.3 0.8 fusion.41
  151.9 755.0 %all-gather.11.cloned.1.call-done = bf16[512,4,384]{2,1,0:T(4,128)(2,1)} async-done(((bf16[1,4,384]{2,1,0:T(4,128)(2,1)}), bf16[512,4,384]{2,1,0:T(4,128)(2,1)}) %all-gather.11.cloned.1.call-update) | async-done | bytes 1572880 | tf_op jit(solution)/shard_map/all_gather | solution.py:139
  906.9 6.0 reshape.250
  912.9 3.2 fusion.75
  916.4 743.0 %all-gather.13.cloned.1.call-done = bf16[512,4,384]{2,1,0:T(4,128)(2,1)} async-done(((bf16[1,4,384]{2,1,0:T(4,128)(2,1)}), bf16[512,4,384]{2,1,0:T(4,128)(2,1)}) %all-gather.13.cloned.1.call-update) | async-done | bytes 1572880 | tf_op jit(solution)/shard_map/all_gather | solution.py:140
  1659.4 6.1 reshape.257
  1665.4 3.1 fusion.38
  1669.3 4.6 fusion.47
  1674.2 1.5 convolution_convert_fusion
  (53 shorter events, 5.9 us)
Async XLA Ops:
  6.5 1667.7 %copy-start = (bf16[384,768]{1,0:T(8,128)(2,1)S(1)}, bf16[384,768]{1,0:T(8,128)(2,1)}, u32[]{:S(2)}) copy-start(bf16[384,768]{1,0:T(8,128)(2,1)} %param.9) | copy-start | bytes 1769476
  6.5 11.1 copy-start.2
  6.5 7.1 copy-start.3
  6.5 74.5 %all-gather.9.cloned.1.call-start = ((), (), s32[]{:S(2)}) async-start(), calls=%async_computation.1 | async-start | bytes 1622016 | tf_op jit(solution)/shard_map/all_gather | solution.py:131
  10.3 7.8 copy-start.4
  10.3 136.7 %all-gather.7.cloned.1.call-start = ((), (), s32[]{:S(2)}) async-start(), calls=%async_computation | async-start | bytes 1622016 | tf_op jit(solution)/shard_map/all_gather | solution.py:130
  11.1 895.8 %all-gather.11.cloned.1.call-start = ((), (), s32[]{:S(2)}) async-start(), calls=%async_computation.2 | async-start | bytes 1575936 | tf_op jit(solution)/shard_map/all_gather | solution.py:139
  16.8 1642.5 %all-gather.13.cloned.1.call-start = ((), (), s32[]{:S(2)}) async-start(), calls=%async_computation.3 | async-start | bytes 1575936 | tf_op jit(solution)/shard_map/all_gather | solution.py:140
  20.6 2.7 copy-start.1
  148.7 1.6 copy-start.5
  151.6 761.3 %copy-start.6 = (bf16[4,384]{0,1:T(8,128)(2,1)S(1)}, bf16[4,384]{0,1:T(8,128)(2,1)}, u32[]{:S(2)}) copy-start(bf16[4,384]{0,1:T(8,128)(2,1)} %get-tuple-element.7) | copy-start | bytes 9220
Sparse Core Ops, SparseCore 0:
  10.4 70.5 all-gather.8
  83.2 63.8 all-gather.6
  149.1 757.6 all-gather.10
  908.9 750.4 all-gather.12
where the time goes:
time: 1680 us
  waiting for transfers between devices  1620 us (96%)
  local copies, waits for them, and re-layouts  25 us (1%)
    all_gather x1, waiting for transfers between devices, on_device(): lax.all_gather(far_k, ('grp', 'seq'), axis=0, tiled=True)  755 us
    all_gather x1, waiting for transfers between devices, on_device(): lax.all_gather(far_v, ('grp', 'seq'), axis=0, tiled=True)  743 us
    all_gather x1, waiting for transfers between devices, on_device(): lax.all_gather(near_k, 'seq', axis=0, tiled=True)  63.3 us
    all_gather x1, waiting for transfers between devices, on_device(): lax.all_gather(near_v, 'seq', axis=0, tiled=True)  57.6 us
  transfers between devices with their start and end apart: 4, of which 4 were waited for; matrix products, arithmetic and copies ran while one was open for 2% of the time, Pallas kernels for 0%

commit v1 on v0

v1 whole, which is shorter than its diff:
```python
import functools
import math

import jax
import jax.numpy as jnp
from jax import lax
from jax.experimental import pallas as pl
from jax.experimental.pallas import tpu as pltpu
from jax.sharding import PartitionSpec as P

MESH = pl.DeviceIdType.MESH
HEADS = 6
HD = 64
TOK = 512
SEQ = 32
GRP = 16
NEG = -1e30
C = math.log2(math.e) / math.sqrt(HD)
F32 = jnp.float32
BF16 = jnp.bfloat16


def nt(a, b):
    return lax.dot_general(a, b, (((1,), (1,)), ((), ())), preferred_element_type=F32)


def nn(a, b):
    return lax.dot_general(a, b, (((1,), (0,)), ((), ())), preferred_element_type=F32)


def tn(a, b):
    return lax.dot_general(a, b, (((0,), (0,)), ((), ())), preferred_element_type=F32)


def iota(shape, dim):
    return lax.broadcasted_iota(jnp.int32, shape, dim)


def onehot(cond):
    return jnp.where(cond, 1.0, 0.0).astype(BF16)


def near_chip(h):
    return (5 * h + 1) % 16


def far_chip(h):
    return (5 * (h + 6) + 1) % 16


def three(x):
    hi = x.astype(BF16).astype(F32)
    rest = x - hi
    mid = rest.astype(BF16).astype(F32)
    return hi, mid, rest - mid


def kernel(
    q_ref, k_ref, v_ref, off_ref, out_ref,
    kv_send, q_send, f_send, kv_in, q_in, f_in, qz, kvt, scr, ret_send, ret_in,
    kvx, fret_send, fret_in, acc, top, tot,
    kv_ss, q_ss, f_ss, kv_rs, q_rs, f_rs, x_ss, x_rs, ret_ss, ret_rs, fret_ss, fret_rs,
):
    s = lax.axis_index("seq")
    g = lax.axis_index("grp")
    chip, core = s // 2, s % 2
    role = ((chip + 15) * 13) % 16
    is_near = role < HEADS
    is_far = (role >= HEADS) & (role < 2 * HEADS) & (core == 0)
    head = role % HEADS
    is_worker = is_near | is_far

    barrier = pltpu.get_barrier_semaphore()

    def hello(target):
        pl.semaphore_signal(barrier, inc=1, device_id={"seq": target}, device_id_type=MESH)

    @pl.when(is_worker)
    def _():
        def step(i, _):
            @pl.when(i != s)
            def _():
                hello(i)
            return 0
        lax.fori_loop(0, SEQ, step, 0)

    @pl.when(jnp.logical_not(is_worker))
    def _():
        for h in range(HEADS):
            hello(2 * far_chip(h))
            hello(2 * near_chip(h))
            hello(2 * near_chip(h) + 1)

    @pl.when(is_far)
    def _():
        def step(i, _):
            pl.semaphore_signal(barrier, inc=1, device_id={"grp": i}, device_id_type=MESH)
            return 0
        lax.fori_loop(0, g, step, 0)

    lane = iota((32, 128), 1)
    low = lane < HD
    low16 = iota((16, 128), 1) < HD
    row16 = iota((16, 128), 0)
    near_diff = iota((32, 256), 1) - 8 * iota((32, 256), 0)
    fr = iota((16, TOK), 0)
    far_diff = jnp.where(fr < 8, iota((16, TOK), 1) - 128 * (fr % 4), -1)

    def turn(x):
        return pltpu.roll(x, HD, 1)

    for p in range(3):
        near_hot = [onehot(near_diff == off_ref[0, 2 * p + e]) for e in range(2)]
        far_hot = [onehot(far_diff == off_ref[1, 2 * p + e]) for e in range(2)]
        picked = []
        for ref in (q_ref, k_ref, v_ref):
            halves = []
            for a in range(2):
                left = jnp.concatenate(near_hot + [f[:, 256 * a:256 * a + 256] for f in far_hot], axis=0)
                halves.append(nn(left, ref[256 * a:256 * a + 256, 128 * p:128 * p + 128]))
            picked.append(halves)
        pq, pk, pv = picked
        for e in range(2):
            h = 2 * p + e
            for a in range(2):
                rk, rv = pk[a][32 * e:32 * e + 32], pv[a][32 * e:32 * e + 32]
                kv = jnp.where(low, rk, turn(rv)) if e == 0 else jnp.where(low, turn(rk), rv)
                kv_send[h, 32 * a:32 * a + 32, :] = kv.astype(BF16)
            r0, r1 = pq[0][32 * e:32 * e + 32], pq[1][32 * e:32 * e + 32]
            qq = jnp.where(low, r0, turn(r1)) if e == 0 else jnp.where(low, turn(r0), r1)
            q_send[h] = qq.astype(BF16)
            lo = 64 + 16 * e
            fq, fk, fv = [x[0][lo:lo + 16] + x[1][lo:lo + 16] for x in (pq, pk, pv)]
            if e == 0:
                fkv, fqz = jnp.where(low16, fk, turn(fv)), fq
            else:
                fkv, fqz = jnp.where(low16, turn(fk), fv), turn(fq)
            tile = jnp.where(row16 < 4, fkv, jnp.where(low16 & (row16 < 8), fqz, 0.0))
            f_send[h] = tile.astype(BF16)

    @pl.when(is_far)
    def _():
        pl.semaphore_wait(barrier, SEQ - 1 + GRP - 1 - g)

    @pl.when(is_near)
    def _():
        pl.semaphore_wait(barrier, SEQ - 1)

    @pl.when(jnp.logical_not(is_worker))
    def _():
        pl.semaphore_wait(barrier, 3 * HEADS)

    def copy(src, dst, ss, rs, target):
        return pltpu.make_async_remote_copy(
            src_ref=src, dst_ref=dst, send_sem=ss, recv_sem=rs, device_id={"seq": target}, device_id_type=MESH
        )

    def send(src, dst, ss, rs, target):
        @pl.when(s == target)
        def _():
            pltpu.make_async_copy(src, dst, rs).start()

        @pl.when(s != target)
        def _():
            copy(src, dst, ss, rs, target).start()

    def sent(src, dst, ss, rs, target):
        @pl.when(s != target)
        def _():
            copy(src, dst, ss, rs, target).wait_send()

    def slot(n, i):
        return pl.ds(pl.multiple_of(n * i, n), n)

    def outgoing(f):
        for h in range(HEADS):
            f(f_send.at[h], f_in.at[slot(16, s)], f_ss.at[h], f_rs.at[s], 2 * far_chip(h))
        for h in range(HEADS):
            for c in range(2):
                f(kv_send.at[h], kv_in.at[slot(64, s)], kv_ss.at[h, c], kv_rs.at[s], 2 * near_chip(h) + c)
            f(q_send.at[h], q_in.at[slot(32, chip)], q_ss.at[h], q_rs.at[chip], 2 * near_chip(h) + core)

    outgoing(send)

    eye = onehot(iota((128, 128), 0) == iota((128, 128), 1))
    causal = iota((256, 256), 0) <= iota((256, 256), 1)
    lane_q = iota((TOK, 128), 1) < HD
    row_v = iota((128, TOK), 0) < HD

    def local_pair(p):
        cols = slice(128 * p, 128 * p + 128)
        kp, qp, vp = k_ref[:, cols], q_ref[:, cols], v_ref[:, cols]
        vt = nt(eye, vp)
        for e in range(2):
            h = 2 * p + e
            mine = lane_q if e == 0 else jnp.logical_not(lane_q)
            qe = jnp.where(mine, qp, jnp.zeros((), BF16))
            mine_v = row_v if e == 0 else jnp.logical_not(row_v)
            ve = jnp.where(mine_v, vt, 1.0).astype(BF16)
            for t in range(2):
                qt = qe[256 * t:256 * t + 256]
                parts = [nt(kp[256 * b:256 * b + 256], qt) for b in range(t + 1)]
                parts[t] = jnp.where(causal, parts[t], NEG)
                m = jnp.max(parts[0], axis=0, keepdims=True)
                for x in parts[1:]:
                    m = jnp.maximum(m, jnp.max(x, axis=0, keepdims=True))
                o = None
                for b, x in enumerate(parts):
                    w = jnp.exp2((x - m) * C).astype(BF16)
                    y = nn(ve[:, 256 * b:256 * b + 256], w)
                    o = y if o is None else o + y
                ts = slice(256 * t, 256 * t + 256)
                acc[64 * h:64 * h + 64, ts] = o[64 * e:64 * e + 64]
                other = 64 * (1 - e)
                tot[h, :, ts] = o[other:other + 1]
                top[h, :, ts] = m * C

    local_pair(0)

    @pl.when(is_far)
    def _():
        def wait(i, _):
            copy(f_in.at[slot(16, i)], f_in.at[slot(16, i)], f_ss.at[0], f_rs.at[i], 0).wait_recv()
            return 0
        lax.fori_loop(0, SEQ, wait, 0)
        i, j = iota((128, TOK), 0), iota((128, TOK), 1)
        base = 16 * (i // 4) + i % 4
        rows = f_in[...]
        kvx[slot(128, g), :] = nn(onehot(j == base), rows).astype(BF16)
        qz[0:128, :] = nn(onehot(j == base + 4), rows).astype(BF16)

        def start(i, _):
            pltpu.make_async_remote_copy(
                src_ref=kvx.at[slot(128, g)], dst_ref=kvx.at[slot(128, g)], send_sem=x_ss.at[i],
                recv_sem=x_rs.at[g], device_id={"grp": i}, device_id_type=MESH,
            ).start()
            return 0
        lax.fori_loop(g + 1, GRP, start, 0)

        def clear(i, _):
            kvx[slot(128, i), :] = jnp.zeros((128, 128), BF16)
            return 0
        lax.fori_loop(g + 1, GRP, clear, 0)

    local_pair(1)
    local_pair(2)

    row_one = iota((128, TOK), 0) < HD
    low1 = iota((1, 128), 1) < HD

    @pl.when(is_near)
    def _():
        def wait(i, _):
            copy(kv_in.at[slot(64, i)], kv_in.at[slot(64, i)], q_ss.at[0], kv_rs.at[i], 0).wait_recv()
            return 0
        lax.fori_loop(0, SEQ, wait, 0)

        def wait_q(i, _):
            copy(q_in.at[slot(32, i)], q_in.at[slot(32, i)], q_ss.at[0], q_rs.at[i], 0).wait_recv()
            return 0
        lax.fori_loop(0, 16, wait_q, 0)
        for j in range(16):
            x = q_in[32 * j:32 * j + 32, :].astype(F32)
            qz[64 * j:64 * j + 32, :] = jnp.where(low, x, 0.0).astype(BF16)
            qz[64 * j + 32:64 * j + 64, :] = jnp.where(low, turn(x), 0.0).astype(BF16)
        for b in range(4):
            x = nt(eye, kv_in[TOK * b:TOK * b + TOK, :])
            kvt[:, TOK * b:TOK * b + TOK] = jnp.where(row_one, 1.0, x).astype(BF16)
        ask = iota((TOK, 256), 1)
        ask = (ask // 64) * 128 + core * 64 + ask % 64
        allowed = iota((TOK, 256), 0) <= ask
        for t in range(4):
            qt = qz[256 * t:256 * t + 256, :]
            m = None
            for b in range(t + 1):
                x = nt(kv_in[TOK * b:TOK * b + TOK, :], qt)
                if b == t:
                    x = jnp.where(allowed, x, NEG)
                scr[TOK * b:TOK * b + TOK, :] = x
                y = jnp.max(x, axis=0, keepdims=True)
                m = y if m is None else jnp.maximum(m, y)
            o = None
            for b in range(t + 1):
                w = jnp.exp2((scr[TOK * b:TOK * b + TOK, :] - m) * C).astype(BF16)
                y = nn(kvt[:, TOK * b:TOK * b + TOK], w)
                o = y if o is None else o + y
            total = o[0:1]
            norm = o[64:128] / total
            lses = three(m * C + jnp.log(total) * math.log2(math.e))
            for jj in range(4):
                j = 4 * t + jj
                cols = slice(128 * (jj // 2), 128 * (jj // 2) + 128)
                top_half, bottom = norm[0:32, cols], norm[32:64, cols]
                ls = [x[:, cols] for x in lses]
                if jj % 2 == 0:
                    packed = jnp.where(low, top_half, turn(bottom))
                else:
                    packed = jnp.where(low, turn(top_half), bottom)
                tail = jnp.where(row16 == 0, ls[0], jnp.where(row16 == 1, ls[1], jnp.where(row16 == 2, ls[2], 0.0)))
                if jj % 2 == 1:
                    tail = turn(tail)
                ret_send[j, 0:32, :] = packed.astype(BF16)
                ret_send[j, 32:48, :] = tail.astype(BF16)
                send(ret_send.at[j], ret_in.at[head], ret_ss.at[j], ret_rs.at[head], 2 * j + core)

    @pl.when(is_far)
    def _():
        def wait(i, _):
            pltpu.make_async_remote_copy(
                src_ref=kvx.at[slot(128, i)], dst_ref=kvx.at[slot(128, i)], send_sem=x_ss.at[i],
                recv_sem=x_rs.at[i], device_id={"grp": i}, device_id_type=MESH,
            ).wait_recv()
            return 0
        lax.fori_loop(0, g, wait, 0)
        qf = qz[0:128, :]
        limit = iota((TOK, 128), 1) + 128 * g
        m = None
        for b in range(4):
            x = nt(kvx[TOK * b:TOK * b + TOK, :], qf)
            x = jnp.where(iota((TOK, 128), 0) + TOK * b <= limit, x, NEG)
            scr[TOK * b:TOK * b + TOK, 0:128] = x
            y = jnp.max(x, axis=0, keepdims=True)
            m = y if m is None else jnp.maximum(m, y)
        o = None
        for b in range(4):
            xt = nt(eye, kvx[TOK * b:TOK * b + TOK, :])
            xt = jnp.where(row_one, 1.0, xt).astype(BF16)
            w = jnp.exp2((scr[TOK * b:TOK * b + TOK, 0:128] - m) * C).astype(BF16)
            y = nn(xt, w)
            o = y if o is None else o + y
        total = o[0:1]
        norm = (o[64:128] / total).astype(BF16)
        ls = three(m * C + jnp.log(total) * math.log2(math.e))
        r = iota((64, 128), 0)
        tail = jnp.where(r == 0, ls[0], jnp.where(r == 1, ls[1], jnp.where(r == 2, ls[2], 0.0)))
        both = jnp.concatenate([norm, tail.astype(BF16)], axis=0)
        i, j = iota((TOK, 128), 0), iota((TOK, 128), 1)
        place = onehot((j == 4 * (i // 16) + i % 16) & (i % 16 < 4))
        fret_send[...] = nt(place, both).astype(BF16)

        def start(i, _):
            send(fret_send.at[slot(16, i)], fret_in.at[head], fret_ss.at[i], fret_rs.at[head], i)
            return 0
        lax.fori_loop(0, SEQ, start, 0)

    spread = iota((128, TOK), 1) - 8 * (iota((128, TOK), 0) % 64)
    tok = iota((1, TOK), 1)
    low48 = iota((48, 128), 1) < HD
    for h in range(HEADS):
        copy(ret_in.at[h], ret_in.at[h], ret_ss.at[0], ret_rs.at[h], 0).wait_recv()
        near_off, far_off = off_ref[0, h], off_ref[1, h]
        x = ret_in[h]
        zero = jnp.zeros((), BF16)
        left = jnp.concatenate([jnp.where(low48, x, zero), jnp.where(low, zero, x[0:32])], axis=0)
        u = nn(left, onehot(spread == near_off))
        l1 = jnp.where(tok % 8 == near_off, u[32:33] + u[33:34] + u[34:35], NEG)
        copy(fret_in.at[h], fret_in.at[h], fret_ss.at[0], fret_rs.at[h], 0).wait_recv()
        w = tn(fret_in[h], onehot(far_diff == far_off))
        l2 = jnp.where(tok % 128 == far_off, w[64:65] + w[65:66] + w[66:67], NEG)
        m0 = top[h]
        big = jnp.maximum(jnp.maximum(m0, l1), l2)
        w0, w1, w2 = jnp.exp2(m0 - big), jnp.exp2(l1 - big), jnp.exp2(l2 - big)
        inv = 1.0 / (w0 * tot[h] + w1 + w2)
        w0, w1, w2 = w0 * inv, w1 * inv, w2 * inv
        for a in range(2):
            rows = slice(64 * h + 32 * a, 64 * h + 32 * a + 32)
            n1 = u[48 * a:48 * a + 32]
            n2 = w[32 * a:32 * a + 32]
            out_ref[rows, :] = (acc[rows, :] * w0 + n1 * w1 + n2 * w2).astype(BF16)

    outgoing(sent)

    @pl.when(is_near)
    def _():
        def step(j, _):
            sent(ret_send.at[j], ret_in.at[head], ret_ss.at[j], ret_rs.at[head], 2 * j + core)
            return 0
        lax.fori_loop(0, 16, step, 0)

    @pl.when(is_far)
    def _():
        def step(i, _):
            sent(fret_send.at[slot(16, i)], fret_in.at[head], fret_ss.at[i], fret_rs.at[head], i)
            return 0
        lax.fori_loop(0, SEQ, step, 0)

        def step_x(i, _):
            pltpu.make_async_remote_copy(
                src_ref=kvx.at[slot(128, g)], dst_ref=kvx.at[slot(128, g)], send_sem=x_ss.at[i],
                recv_sem=x_rs.at[g], device_id={"grp": i}, device_id_type=MESH,
            ).wait_send()
            return 0
        lax.fori_loop(g + 1, GRP, step_x, 0)


def on_device(queries, keys, values, offsets, out_weight):
    vm = pl.BlockSpec(memory_space=pltpu.VMEM)
    dma = pltpu.SemaphoreType.DMA
    merged = pl.pallas_call(
        kernel,
        out_shape=jax.ShapeDtypeStruct((HEADS * HD, TOK), BF16),
        in_specs=[vm, vm, vm, pl.BlockSpec(memory_space=pltpu.SMEM)],
        out_specs=vm,
        scratch_shapes=[
            pltpu.VMEM((HEADS, 64, 128), BF16),
            pltpu.VMEM((HEADS, 32, 128), BF16),
            pltpu.VMEM((HEADS, 16, 128), BF16),
            pltpu.VMEM((2048, 128), BF16),
            pltpu.VMEM((512, 128), BF16),
            pltpu.VMEM((512, 128), BF16),
            pltpu.VMEM((1024, 128), BF16),
            pltpu.VMEM((128, 2048), BF16),
            pltpu.VMEM((2048, 256), F32),
            pltpu.VMEM((16, 48, 128), BF16),
            pltpu.VMEM((HEADS, 48, 128), BF16),
            pltpu.VMEM((2048, 128), BF16),
            pltpu.VMEM((512, 128), BF16),
            pltpu.VMEM((HEADS, 16, 128), BF16),
            pltpu.VMEM((HEADS * HD, TOK), F32),
            pltpu.VMEM((HEADS, 1, TOK), F32),
            pltpu.VMEM((HEADS, 1, TOK), F32),
            dma((HEADS, 2)), dma((HEADS,)), dma((HEADS,)),
            dma((SEQ,)), dma((16,)), dma((SEQ,)),
            dma((GRP,)), dma((GRP,)),
            dma((16,)), dma((HEADS,)),
            dma((SEQ,)), dma((HEADS,)),
        ],
        compiler_params=pltpu.CompilerParams(
            collective_id=0, has_side_effects=True, vmem_limit_bytes=48 * 1024 * 1024
        ),
    )(queries, keys, values, offsets)
    return tn(merged, out_weight).astype(BF16)


def solution(mesh):
    placed = (P(("grp", "seq"), None), P(("grp", "seq"), None), P(("grp", "seq"), None), P(), P())
    return jax.shard_map(
        on_device, mesh=mesh, in_specs=placed, out_specs=P(("grp", "seq"), None), check_vma=False
    )
```

time: 1680 us -> 44.4 us (0.03)
  the two profiles are of different devices: /device:TPU:1 before, /device:TPU:135 now
where the time goes in v1:
time: 44.4 us; the launch traced here: 44.2 us
  Pallas kernels  38.9 us (88%)
  local copies, waits for them, and re-layouts  3.73 us (8%)
  matrix products  1.48 us (3%)
    pallas_call x1, Pallas kernels, on_device(): pl.pallas_call(kernel, out_shape=jax.ShapeDtypeStruct((HEADS * HD, TOK),...  38.9 us
    unnamed x10, local copies, waits for them, and re-layouts  3.73 us
    dot_general x1, matrix products, tn(): lax.dot_general(a, b, (((0,), (0,)), ((), ())), preferred_element_type=F32)  1.48 us

profile of v1, /device:TPU:135, one launch (start us, length us, event | category | flops | bytes accessed | tf_op | source)
XLA Modules:
  0.0 44.2 jit_solution(166330155950496875)
XLA Ops:
  0.0 0.0 copy-start
  0.0 0.0 copy-start.1
  0.0 1.1 %copy-done.1 = bf16[512,384]{1,0:T(8,128)(2,1)S(1)} copy-done((bf16[512,384]{1,0:T(8,128)(2,1)S(1)}, bf16[512,384]{1,0:T(8,128)(2,1)}, u32[]{:S(2)}) %copy-start.1) | copy-done | bytes 393240
  1.1 0.0 copy-start.2
  1.1 1.0 %copy-done.2 = bf16[512,384]{1,0:T(8,128)(2,1)S(1)} copy-done((bf16[512,384]{1,0:T(8,128)(2,1)S(1)}, bf16[512,384]{1,0:T(8,128)(2,1)}, u32[]{:S(2)}) %copy-start.2) | copy-done | bytes 393240
  2.1 0.0 copy-start.3
  2.1 1.0 %copy-done.3 = bf16[512,384]{1,0:T(8,128)(2,1)S(1)} copy-done((bf16[512,384]{1,0:T(8,128)(2,1)S(1)}, bf16[512,384]{1,0:T(8,128)(2,1)}, u32[]{:S(2)}) %copy-start.3) | copy-done | bytes 393240
  3.1 0.0 copy-start.4
  3.1 0.7 %copy-done.4 = s32[2,6]{1,0:T(2,128)S(1)} copy-done((s32[2,6]{1,0:T(2,128)S(1)}, s32[2,6]{1,0:T(2,128)}, u32[]{:S(2)}) %copy-start.4) | copy-done | bytes 72
  3.7 38.9 %shard_map.55 = bf16[384,512]{1,0:T(8,128)(2,1)S(1)} custom-call(bf16[512,384]{1,0:T(8,128)(2,1)S(1)} %copy-done.1, bf16[512,384]{1,0:T(8,128)(2,1)S(1)} %copy-done.2, bf16[512,384]{1,0:T(8,128)(2,1)S(1)} %copy-done.3, s32[2,6]{1,0:T(2,128)S(1)} %copy-done.4), custom_call_target="tpu_custom_call" | custom-call | tf_op jit(solution)/shard_map/pallas_call | solution.py:399
  42.7 0.0 copy-done
  42.7 1.5 %convolution_convert_fusion = bf16[512,768]{1,0:T(8,128)(2,1)} fusion(bf16[384,512]{1,0:T(8,128)(2,1)S(1)} %shard_map.55, bf16[384,768]{1,0:T(8,128)(2,1)S(1)} %copy-done), kind=kOutput, calls=%fused_computation | convolution fusion | flops 302383104 | bytes 1769472 | tf_op jit(solution)/shard_map/dot_general | solution.py:32
Async XLA Ops:
  0.0 42.7 %copy-start = (bf16[384,768]{1,0:T(8,128)(2,1)S(1)}, bf16[384,768]{1,0:T(8,128)(2,1)}, u32[]{:S(2)}) copy-start(bf16[384,768]{1,0:T(8,128)(2,1)} %param.9) | copy-start | bytes 1769476
  0.0 1.1 %copy-start.1 = (bf16[512,384]{1,0:T(8,128)(2,1)S(1)}, bf16[512,384]{1,0:T(8,128)(2,1)}, u32[]{:S(2)}) copy-start(bf16[512,384]{1,0:T(8,128)(2,1)} %q_ref.1) | copy-start | bytes 1179652
  1.1 1.0 %copy-start.2 = (bf16[512,384]{1,0:T(8,128)(2,1)S(1)}, bf16[512,384]{1,0:T(8,128)(2,1)}, u32[]{:S(2)}) copy-start(bf16[512,384]{1,0:T(8,128)(2,1)} %k_ref.1) | copy-start | bytes 1179652
  2.1 1.0 %copy-start.3 = (bf16[512,384]{1,0:T(8,128)(2,1)S(1)}, bf16[512,384]{1,0:T(8,128)(2,1)}, u32[]{:S(2)}) copy-start(bf16[512,384]{1,0:T(8,128)(2,1)} %v_ref.1) | copy-start | bytes 1179652
  3.1 0.7 %copy-start.4 = (s32[2,6]{1,0:T(2,128)S(1)}, s32[2,6]{1,0:T(2,128)}, u32[]{:S(2)}) copy-start(s32[2,6]{1,0:T(2,128)} %off_ref.1) | copy-start | bytes 148

commit v2 on v1

v2 whole, which is shorter than its diff:
```python
import math

import jax
import jax.numpy as jnp
from jax import lax
from jax.experimental import pallas as pl
from jax.experimental.pallas import tpu as pltpu
from jax.sharding import PartitionSpec as P

MESH = pl.DeviceIdType.MESH
HEADS = 6
HD = 64
TOK = 512
SEQ = 32
GRP = 16
NEG = -1e30
C = math.log2(math.e) / math.sqrt(HD)
F32 = jnp.float32
BF16 = jnp.bfloat16


def nt(a, b):
    return lax.dot_general(a, b, (((1,), (1,)), ((), ())), preferred_element_type=F32)


def nn(a, b):
    return lax.dot_general(a, b, (((1,), (0,)), ((), ())), preferred_element_type=F32)


def tn(a, b):
    return lax.dot_general(a, b, (((0,), (0,)), ((), ())), preferred_element_type=F32)


def iota(shape, dim):
    return lax.broadcasted_iota(jnp.int32, shape, dim)


def onehot(cond):
    return jnp.where(cond, 1.0, 0.0).astype(BF16)


def near_chip(h):
    return (5 * h + 1) % 16


def far_chip(h):
    return (5 * (h + 6) + 1) % 16


def turn(x):
    return pltpu.roll(x, HD, 1)


def three(x):
    hi = x.astype(BF16).astype(F32)
    rest = x - hi
    mid = rest.astype(BF16).astype(F32)
    return hi, mid, rest - mid


def loop(lo, hi, f):
    def step(i, c):
        f(i)
        return c

    lax.fori_loop(lo, hi, step, 0)


def kernel(
    q_hbm, k_hbm, v_hbm, off_hbm, out_ref,
    q_ref, k_ref, v_ref, off_ref,
    n_send, f_send, n_in, o_in, f_in, qz, kvt, scr, ret_send, ret_in,
    kvx, fret_send, fret_in, acc, top, tot, spread, far_hot,
    in_sem, out_ss, n_rs, o_rs, f_rs, z_ss, x_ss, fw_ss, blk_rs, go, ret_ss, ret_rs, fret_rs,
):
    s = lax.axis_index("seq")
    g = lax.axis_index("grp")
    chip, core = s // 2, s % 2
    zh, gx = g // 4, g % 4
    role = ((chip + 15) * 13) % 16
    is_near = role < HEADS
    on_far = (role >= HEADS) & (role < 2 * HEADS)
    is_far = on_far & (core == 0)
    head = role % HEADS
    sibling = s + 1 - 2 * core

    inputs = [
        pltpu.make_async_copy(src, dst, in_sem.at[i])
        for i, (src, dst) in enumerate(
            ((off_hbm, off_ref), (q_hbm, q_ref), (k_hbm, k_ref), (v_hbm, v_ref))
        )
    ]
    for c in inputs:
        c.start()

    barrier = pltpu.get_barrier_semaphore()

    def hello(axis, target):
        pl.semaphore_signal(barrier, inc=1, device_id={axis: target}, device_id_type=MESH)

    @pl.when(is_near | is_far)
    def _():
        def step(i):
            part = ((i // 2 + 15) * 13) % 16
            skip = (part >= HEADS) & (part < 2 * HEADS) & (i % 2 == 0)

            @pl.when((i != s) & jnp.logical_not(skip))
            def _():
                hello("seq", i)
        loop(0, SEQ, step)

    @pl.when(is_far)
    def _():
        for i in range(1, 4):
            hello("grp", 4 * zh + (gx + i) % 4)
        loop(0, zh, lambda z: hello("grp", 4 * z + gx))

    low = iota((32, 128), 1) < HD
    low16 = iota((16, 128), 1) < HD
    row16 = iota((16, 128), 0)
    near_diff = iota((32, 256), 1) - 8 * iota((32, 256), 0)
    fr = iota((16, TOK), 0)
    far_diff = jnp.where(fr < 8, iota((16, TOK), 1) - 128 * (fr % 4), -1)
    for c in inputs:
        c.wait()
    for p in range(3):
        near_hot = [onehot(near_diff == off_ref[0, 2 * p + e]) for e in range(2)]
        hot = [onehot(far_diff == off_ref[1, 2 * p + e]) for e in range(2)]
        for e in range(2):
            far_hot[2 * p + e] = hot[e]
        picked = []
        for ref in (q_ref, k_ref, v_ref):
            halves = []
            for a in range(2):
                left = jnp.concatenate(near_hot + [f[:, 256 * a:256 * a + 256] for f in hot], axis=0)
                halves.append(nn(left, ref[256 * a:256 * a + 256, 128 * p:128 * p + 128]))
            picked.append(halves)
        pq, pk, pv = picked
        for e in range(2):
            h = 2 * p + e
            for a in range(2):
                rk, rv = pk[a][32 * e:32 * e + 32], pv[a][32 * e:32 * e + 32]
                kv = jnp.where(low, rk, turn(rv)) if e == 0 else jnp.where(low, turn(rk), rv)
                n_send[h, 32 * a:32 * a + 32, :] = kv.astype(BF16)
            r0, r1 = pq[0][32 * e:32 * e + 32], pq[1][32 * e:32 * e + 32]
            qq = jnp.where(low, r0, turn(r1)) if e == 0 else jnp.where(low, turn(r0), r1)
            n_send[h, 64:96, :] = qq.astype(BF16)
            lo = 64 + 16 * e
            fq, fk, fv = [x[0][lo:lo + 16] + x[1][lo:lo + 16] for x in (pq, pk, pv)]
            if e == 0:
                fkv, fqz = jnp.where(low16, fk, turn(fv)), fq
            else:
                fkv, fqz = jnp.where(low16, turn(fk), fv), turn(fq)
            tile = jnp.where(row16 < 4, fkv, jnp.where(low16 & (row16 < 8), fqz, 0.0))
            f_send[h] = tile.astype(BF16)

    @pl.when(is_near)
    def _():
        pl.semaphore_wait(barrier, 3 * HEADS - 1)

    @pl.when(jnp.logical_not(is_near | is_far))
    def _():
        pl.semaphore_wait(barrier, 3 * HEADS)

    @pl.when(on_far & (core == 1))
    def _():
        pl.semaphore_signal(go, inc=1, device_id={"seq": sibling}, device_id_type=MESH)

    @pl.when(is_far)
    def _():
        pl.semaphore_wait(go, 1)

    def copy(src, dst, ss, rs, target, axis="seq"):
        return pltpu.make_async_remote_copy(
            src_ref=src, dst_ref=dst, send_sem=ss, recv_sem=rs, device_id={axis: target}, device_id_type=MESH
        )

    def send(src, dst, ss, rs, target):
        @pl.when(s == target)
        def _():
            pltpu.make_async_copy(src, dst, rs).start()

        @pl.when(s != target)
        def _():
            copy(src, dst, ss, rs, target).start()

    def arrived(dst, rs):
        copy(dst, dst, in_sem.at[0], rs, sibling).wait_recv()

    def sent(src, ss):
        copy(src, src, ss, in_sem.at[0], sibling).wait_send()

    for i in range(HEADS):
        h = (chip + i) % HEADS
        send(f_send.at[h], f_in.at[s], out_ss.at[0], f_rs, 2 * far_chip(h))
    for i in range(HEADS):
        h = (chip + i) % HEADS
        send(n_send.at[h], n_in.at[chip], out_ss.at[1], n_rs.at[chip // 4], 2 * near_chip(h) + core)
    for i in range(HEADS):
        h = (chip + i) % HEADS
        copy(
            n_send.at[h, pl.ds(0, 64)], o_in.at[chip], out_ss.at[2], o_rs.at[chip // 4], 2 * near_chip(h) + 1 - core
        ).start()

    eye = onehot(iota((128, 128), 0) == iota((128, 128), 1))
    causal = iota((256, 256), 0) <= iota((256, 256), 1)
    lane_q = iota((TOK, 128), 1) < HD
    row_v = iota((128, TOK), 0) < HD
    row_one = iota((128, 256), 0) < HD

    def local_pair(p):
        cols = slice(128 * p, 128 * p + 128)
        kp, qp, vp = k_ref[:, cols], q_ref[:, cols], v_ref[:, cols]
        vt = nt(eye, vp)
        for e in range(2):
            h = 2 * p + e
            mine = lane_q if e == 0 else jnp.logical_not(lane_q)
            qe = jnp.where(mine, qp, jnp.zeros((), BF16))
            mine_v = row_v if e == 0 else jnp.logical_not(row_v)
            ve = jnp.where(mine_v, vt, 1.0).astype(BF16)
            for t in range(2):
                qt = qe[256 * t:256 * t + 256]
                parts = [nt(kp[256 * b:256 * b + 256], qt) for b in range(t + 1)]
                parts[t] = jnp.where(causal, parts[t], NEG)
                m = jnp.max(parts[0], axis=0, keepdims=True)
                for x in parts[1:]:
                    m = jnp.maximum(m, jnp.max(x, axis=0, keepdims=True))
                o = None
                for b, x in enumerate(parts):
                    w = jnp.exp2((x - m) * C).astype(BF16)
                    y = nn(ve[:, 256 * b:256 * b + 256], w)
                    o = y if o is None else o + y
                ts = slice(256 * t, 256 * t + 256)
                acc[64 * h:64 * h + 64, ts] = o[64 * e:64 * e + 64]
                other = 64 * (1 - e)
                tot[h, :, ts] = o[other:other + 1]
                top[h, :, ts] = m * C

    def to_z(z):
        return copy(kvx.at[g], kvx.at[g], z_ss.at[z], blk_rs.at[g], 4 * z + gx, "grp")

    def to_x(b, ss, x):
        return copy(kvx.at[b], kvx.at[b], ss, blk_rs.at[b], 4 * zh + x, "grp")

    for p in range(3):
        local_pair(p)

    @pl.when(is_far)
    def _():
        def clear(b):
            kvx[b] = jnp.zeros((128, 128), BF16)
        loop(g + 1, GRP, clear)
        arrived(f_in, f_rs)
        i, j = iota((128, TOK), 0), iota((128, TOK), 1)
        base = 16 * (i // 4) + i % 4
        rows = f_in[...].reshape(TOK, 128)
        kvx[g] = nn(onehot(j == base), rows).astype(BF16)
        qz[...] = nn(onehot(j == base + 4), rows).astype(BF16)
        pl.semaphore_wait(barrier, 6 - zh)
        loop(zh + 1, 4, lambda z: to_z(z).start())
        loop(gx + 1, 4, lambda x: to_x(g, x_ss.at[x], x).start())

        def step(z):
            b = 4 * z + gx
            arrived(kvx.at[b], blk_rs.at[b])
            for i in range(1, 4):
                to_x(b, fw_ss.at[z, i - 1], (gx + i) % 4).start()
        loop(0, zh, step)

    for h in range(HEADS):
        spread[h] = onehot(iota((128, TOK), 1) - 8 * (iota((128, TOK), 0) % 64) == off_ref[0, h])

    @pl.when(is_near)
    def _():
        inner = iota((256, 256), 0) // 64 < iota((256, 256), 1) // 64 + core
        for t in range(4):
            arrived(n_in.at[pl.ds(4 * t, 4)], n_rs.at[t])
            arrived(o_in.at[pl.ds(4 * t, 4)], o_rs.at[t])

            def part(b, side):
                x = n_in[4 * b:4 * b + 4, 0:64, :] if side == 0 else o_in[4 * b:4 * b + 4]
                return x.reshape(256, 128)

            for side in range(2):
                x = nt(eye, part(t, side))
                kvt[2 * t + side] = jnp.where(row_one, 1.0, x).astype(BF16)
            asks = []
            for i in range(4 * t, 4 * t + 4):
                x = n_in[i, 64:96, :].astype(F32)
                asks += [jnp.where(low, x, 0.0), jnp.where(low, turn(x), 0.0)]
            qt = jnp.concatenate(asks, axis=0).astype(BF16)
            m = None
            for n in range(2 * t + 2):
                x = nt(part(n // 2, n % 2), qt)
                if n // 2 == t:
                    x = jnp.where(causal if n % 2 == 0 else inner, x, NEG)
                scr[n] = x
                y = jnp.max(x, axis=0, keepdims=True)
                m = y if m is None else jnp.maximum(m, y)
            o = None
            for n in range(2 * t + 2):
                w = jnp.exp2((scr[n] - m) * C).astype(BF16)
                y = nn(kvt[n], w)
                o = y if o is None else o + y
            total = o[0:1]
            norm = o[64:128] / total
            lses = three(m * C + jnp.log(total) * math.log2(math.e))
            for jj in range(4):
                j = 4 * t + jj
                cols = slice(128 * (jj // 2), 128 * (jj // 2) + 128)
                top_half, bottom = norm[0:32, cols], norm[32:64, cols]
                ls = [x[:, cols] for x in lses]
                if jj % 2 == 0:
                    packed = jnp.where(low, top_half, turn(bottom))
                else:
                    packed = jnp.where(low, turn(top_half), bottom)
                tail = jnp.where(row16 == 0, ls[0], jnp.where(row16 == 1, ls[1], jnp.where(row16 == 2, ls[2], 0.0)))
                if jj % 2 == 1:
                    tail = turn(tail)
                ret_send[j, 0:32, :] = packed.astype(BF16)
                ret_send[j, 32:48, :] = tail.astype(BF16)
                send(ret_send.at[j], ret_in.at[head], ret_ss.at[0], ret_rs.at[head], 2 * j + core)

    @pl.when(is_far)
    def _():
        def step(b):
            @pl.when(b % 4 != gx)
            def _():
                arrived(kvx.at[b], blk_rs.at[b])
        loop(0, g, step)
        qf = qz[...]
        limit = iota((TOK, 128), 1) + 128 * g
        row = iota((TOK, 128), 0)

        def part(b):
            return kvx[4 * b:4 * b + 4].reshape(TOK, 128)

        m = None
        xs = []
        for b in range(4):
            x = nt(part(b), qf)
            x = jnp.where(row + TOK * b <= limit, x, NEG)
            xs.append(x)
            y = jnp.max(x, axis=0, keepdims=True)
            m = y if m is None else jnp.maximum(m, y)
        o = None
        for b in range(4):
            xt = nt(eye, part(b))
            xt = jnp.where(row_v, 1.0, xt).astype(BF16)
            y = nn(xt, jnp.exp2((xs[b] - m) * C).astype(BF16))
            o = y if o is None else o + y
        total = o[0:1]
        norm = (o[64:128] / total).astype(BF16)
        ls = three(m * C + jnp.log(total) * math.log2(math.e))
        r = iota((64, 128), 0)
        tail = jnp.where(r == 0, ls[0], jnp.where(r == 1, ls[1], jnp.where(r == 2, ls[2], 0.0)))
        both = jnp.concatenate([norm, tail.astype(BF16)], axis=0)
        i, j = iota((TOK, 128), 0), iota((TOK, 128), 1)
        place = onehot((j == 4 * (i // 16) + i % 16) & (i % 16 < 4))
        fret_send[...] = nt(place, both).astype(BF16).reshape(SEQ, 16, 128)
        loop(0, SEQ, lambda i: send(fret_send.at[i], fret_in.at[head], ret_ss.at[1], fret_rs.at[head], i))

    tok = iota((1, TOK), 1)
    low48 = iota((48, 128), 1) < HD
    zero = jnp.zeros((), BF16)
    for h in range(HEADS):
        arrived(ret_in.at[h], ret_rs.at[h])
        x = ret_in[h]
        left = jnp.concatenate([jnp.where(low48, x, zero), jnp.where(low, zero, x[0:32])], axis=0)
        u = nn(left, spread[h])
        l1 = jnp.where(tok % 8 == off_ref[0, h], u[32:33] + u[33:34] + u[34:35], NEG)
        arrived(fret_in.at[h], fret_rs.at[h])
        w = tn(fret_in[h], far_hot[h])
        l2 = jnp.where(tok % 128 == off_ref[1, h], w[64:65] + w[65:66] + w[66:67], NEG)
        m0 = top[h]
        big = jnp.maximum(jnp.maximum(m0, l1), l2)
        w0, w1, w2 = jnp.exp2(m0 - big), jnp.exp2(l1 - big), jnp.exp2(l2 - big)
        inv = 1.0 / (w0 * tot[h] + w1 + w2)
        w0, w1, w2 = w0 * inv, w1 * inv, w2 * inv
        for a in range(2):
            rows = slice(64 * h + 32 * a, 64 * h + 32 * a + 32)
            n1 = u[48 * a:48 * a + 32]
            n2 = w[32 * a:32 * a + 32]
            out_ref[rows, :] = (acc[rows, :] * w0 + n1 * w1 + n2 * w2).astype(BF16)

    sent(n_send.at[:, pl.ds(0, 64)], out_ss.at[2])

    @pl.when(is_near)
    def _():
        sent(n_send.at[pl.ds(0, HEADS - 1)], out_ss.at[1])
        sent(ret_send.at[pl.ds(0, 15)], ret_ss.at[0])

    @pl.when(jnp.logical_not(is_near))
    def _():
        sent(n_send, out_ss.at[1])

    @pl.when(is_far)
    def _():
        sent(f_send.at[pl.ds(0, HEADS - 1)], out_ss.at[0])
        sent(fret_send.at[pl.ds(0, SEQ - 1)], ret_ss.at[1])
        loop(gx + 1, 4, lambda x: to_x(g, x_ss.at[x], x).wait_send())
        loop(zh + 1, 4, lambda z: to_z(z).wait_send())

        def step(z):
            for i in range(1, 4):
                to_x(4 * z + gx, fw_ss.at[z, i - 1], (gx + i) % 4).wait_send()
        loop(0, zh, step)

    @pl.when(jnp.logical_not(is_far))
    def _():
        sent(f_send, out_ss.at[0])


def on_device(queries, keys, values, offsets, out_weight):
    hbm = pl.BlockSpec(memory_space=pltpu.HBM)
    vm = pltpu.VMEM
    dma = pltpu.SemaphoreType.DMA
    merged = pl.pallas_call(
        kernel,
        out_shape=jax.ShapeDtypeStruct((HEADS * HD, TOK), BF16),
        in_specs=[hbm, hbm, hbm, hbm],
        out_specs=pl.BlockSpec(memory_space=pltpu.VMEM),
        scratch_shapes=[
            vm((TOK, HEADS * HD), BF16),
            vm((TOK, HEADS * HD), BF16),
            vm((TOK, HEADS * HD), BF16),
            pltpu.SMEM((2, HEADS), jnp.int32),
            vm((HEADS, 96, 128), BF16),
            vm((HEADS, 16, 128), BF16),
            vm((16, 96, 128), BF16),
            vm((16, 64, 128), BF16),
            vm((SEQ, 16, 128), BF16),
            vm((128, 128), BF16),
            vm((8, 128, 256), BF16),
            vm((8, 256, 256), F32),
            vm((16, 48, 128), BF16),
            vm((HEADS, 48, 128), BF16),
            vm((GRP, 128, 128), BF16),
            vm((SEQ, 16, 128), BF16),
            vm((HEADS, 16, 128), BF16),
            vm((HEADS * HD, TOK), F32),
            vm((HEADS, 1, TOK), F32),
            vm((HEADS, 1, TOK), F32),
            vm((HEADS, 128, TOK), BF16),
            vm((HEADS, 16, TOK), BF16),
            dma((4,)), dma((3,)), dma((4,)), dma((4,)), dma,
            dma((4,)), dma((4,)), dma((3, 3)), dma((GRP,)),
            pltpu.SemaphoreType.REGULAR,
            dma((2,)), dma((HEADS,)), dma((HEADS,)),
        ],
        compiler_params=pltpu.CompilerParams(
            collective_id=0, has_side_effects=True, vmem_limit_bytes=56 * 1024 * 1024
        ),
    )(queries, keys, values, offsets)
    return tn(merged, out_weight).astype(BF16)


def solution(mesh):
    placed = (P(("grp", "seq"), None), P(("grp", "seq"), None), P(("grp", "seq"), None), P(), P())
    return jax.shard_map(
        on_device, mesh=mesh, in_specs=placed, out_specs=P(("grp", "seq"), None), check_vma=False
    )
```

time: 44.4 us -> 35.4 us (0.80)
  the two profiles are of different devices: /device:TPU:135 before, /device:TPU:385 now
where the time goes in v2:
time: 35.4 us; the launch traced here: 35.3 us
  Pallas kernels  32.8 us (93%)
  matrix products  2.47 us (7%)
    pallas_call x1, Pallas kernels, on_device(): pl.pallas_call(kernel, out_shape=jax.ShapeDtypeStruct((HEADS * HD, TOK),...  32.8 us
    dot_general x1, matrix products, tn(): lax.dot_general(a, b, (((0,), (0,)), ((), ())), preferred_element_type=F32)  2.47 us

profile of v2, /device:TPU:385, one launch (start us, length us, event | category | flops | bytes accessed | tf_op | source)
XLA Modules:
  0.0 35.3 jit_solution(12891922149712429498)
XLA Ops:
  0.0 0.0 copy-start
  0.0 32.8 %shard_map.55 = bf16[384,512]{1,0:T(8,128)(2,1)} custom-call(bf16[512,384]{1,0:T(8,128)(2,1)} %q_hbm.1, bf16[512,384]{1,0:T(8,128)(2,1)} %k_hbm.1, bf16[512,384]{1,0:T(8,128)(2,1)} %v_hbm.1, s32[2,6]{1,0:T(2,128)} %off_hbm.1), custom_call_target="tpu_custom_call" | custom-call | tf_op jit(solution)/shard_map/pallas_call | solution.py:418
  32.8 0.0 copy-done
  32.8 2.5 %convolution_convert_fusion = bf16[512,768]{1,0:T(8,128)(2,1)} fusion(bf16[384,512]{1,0:T(8,128)(2,1)} %shard_map.55, bf16[384,768]{1,0:T(8,128)(2,1)S(1)} %copy-done), kind=kOutput, calls=%fused_computation | convolution fusion | flops 302383104 | bytes 1769472 | tf_op jit(solution)/shard_map/dot_general | solution.py:31
Async XLA Ops:
  0.0 32.8 %copy-start = (bf16[384,768]{1,0:T(8,128)(2,1)S(1)}, bf16[384,768]{1,0:T(8,128)(2,1)}, u32[]{:S(2)}) copy-start(bf16[384,768]{1,0:T(8,128)(2,1)} %param.9) | copy-start | bytes 1769476

commit v3 on v2

--- a/solution.py
+++ b/solution.py
@@ -69,9 +69,9 @@
 def kernel(
     q_hbm, k_hbm, v_hbm, off_hbm, out_ref,
     q_ref, k_ref, v_ref, off_ref,
-    n_send, f_send, n_in, o_in, f_in, qz, kvt, scr, ret_send, ret_in,
-    kvx, fret_send, fret_in, acc, top, tot, spread, far_hot,
-    in_sem, out_ss, n_rs, o_rs, f_rs, z_ss, x_ss, fw_ss, blk_rs, go, ret_ss, ret_rs, fret_rs,
+    n_send, f_send, n_in, o_in, f_in, g_in, qz, kvt, scr, ret_send, ret_in,
+    kvx, fret_send, fret_in, acc, top, tot, spread, far_hot, far_m, far_o,
+    in_sem, out_ss, n_rs, o_rs, f_rs, g_rs, z_ss, x_ss, blk_rs, go, ret_ss, ret_rs, fret_rs,
 ):
     s = lax.axis_index("seq")
     g = lax.axis_index("grp")
@@ -95,16 +95,17 @@
 
     barrier = pltpu.get_barrier_semaphore()
 
+    def far_seat(i):
+        part = ((i // 2 + 15) * 13) % 16
+        return (part >= HEADS) & (part < 2 * HEADS) & (i % 2 == 0) & (zh < 2)
+
     def hello(axis, target):
         pl.semaphore_signal(barrier, inc=1, device_id={axis: target}, device_id_type=MESH)
 
     @pl.when(is_near | is_far)
     def _():
         def step(i):
-            part = ((i // 2 + 15) * 13) % 16
-            skip = (part >= HEADS) & (part < 2 * HEADS) & (i % 2 == 0)
-
-            @pl.when((i != s) & jnp.logical_not(skip))
+            @pl.when((i != s) & jnp.logical_not(far_seat(i)))
             def _():
                 hello("seq", i)
         loop(0, SEQ, step)
@@ -112,8 +113,22 @@
     @pl.when(is_far)
     def _():
         for i in range(1, 4):
-            hello("grp", 4 * zh + (gx + i) % 4)
-        loop(0, zh, lambda z: hello("grp", 4 * z + gx))
+            pl.semaphore_signal(
+                barrier, inc=1, device_id={"grp": 4 * zh + (gx + i) % 4, "seq": sibling}, device_id_type=MESH
+            )
+
+        @pl.when((zh == 1) | (zh == 2))
+        def _():
+            hello("grp", g - 4)
+
+        @pl.when(zh == 3)
+        def _():
+            hello("grp", g - 12)
+            hello("grp", g - 8)
+
+            loop(0, SEQ, lambda i: pl.semaphore_signal(
+                barrier, inc=1, device_id={"grp": g - 4, "seq": i}, device_id_type=MESH
+            ))
 
     low = iota((32, 128), 1) < HD
     low16 = iota((16, 128), 1) < HD
@@ -154,19 +169,22 @@
             tile = jnp.where(row16 < 4, fkv, jnp.where(low16 & (row16 < 8), fqz, 0.0))
             f_send[h] = tile.astype(BF16)
 
-    @pl.when(is_near)
-    def _():
-        pl.semaphore_wait(barrier, 3 * HEADS - 1)
-
-    @pl.when(jnp.logical_not(is_near | is_far))
-    def _():
-        pl.semaphore_wait(barrier, 3 * HEADS)
+    ahead = jnp.where(zh == 2, HEADS, 0)
+
+    @pl.when(is_near | (is_far & (zh > 1)))
+    def _():
+        pl.semaphore_wait(barrier, 3 * HEADS - 1 + ahead)
+
+    @pl.when(jnp.logical_not(is_near | on_far))
+    def _():
+        pl.semaphore_wait(barrier, 3 * HEADS + ahead)
 
     @pl.when(on_far & (core == 1))
     def _():
+        pl.semaphore_wait(barrier, 3 * HEADS + 3 + ahead)
         pl.semaphore_signal(go, inc=1, device_id={"seq": sibling}, device_id_type=MESH)
 
-    @pl.when(is_far)
+    @pl.when(is_far & (zh < 2))
     def _():
         pl.semaphore_wait(go, 1)
 
@@ -193,6 +211,17 @@
     for i in range(HEADS):
         h = (chip + i) % HEADS
         send(f_send.at[h], f_in.at[s], out_ss.at[0], f_rs, 2 * far_chip(h))
+    def early(h):
+        return pltpu.make_async_remote_copy(
+            src_ref=f_send.at[h], dst_ref=g_in.at[s], send_sem=out_ss.at[3], recv_sem=g_rs,
+            device_id={"grp": g + 4, "seq": 2 * far_chip(h)}, device_id_type=MESH,
+        )
+
+    @pl.when(zh == 2)
+    def _():
+        for i in range(HEADS):
+            early((chip + i) % HEADS).start()
+
     for i in range(HEADS):
         h = (chip + i) % HEADS
         send(n_send.at[h], n_in.at[chip], out_ss.at[1], n_rs.at[chip // 4], 2 * near_chip(h) + core)
@@ -236,11 +265,17 @@
                 tot[h, :, ts] = o[other:other + 1]
                 top[h, :, ts] = m * C
 
-    def to_z(z):
-        return copy(kvx.at[g], kvx.at[g], z_ss.at[z], blk_rs.at[g], 4 * z + gx, "grp")
-
-    def to_x(b, ss, x):
-        return copy(kvx.at[b], kvx.at[b], ss, blk_rs.at[b], 4 * zh + x, "grp")
+    def to_group(b, ss, i):
+        return copy(kvx.at[b], kvx.at[b], ss, blk_rs.at[b], i, "grp")
+
+    def on_z(i):
+        return to_group(g, z_ss.at[i], jnp.where((zh == 0) & (i == 1), g + 12, g + 4 + 4 * i))
+
+    def on_z_pass():
+        return to_group(gx, z_ss.at[2], g + 4)
+
+    def on_x(b, i):
+        return to_group(b, x_ss.at[b // 4, i - 1], 4 * zh + (gx + i) % 4)
 
     for p in range(3):
         local_pair(p)
@@ -249,23 +284,46 @@
     def _():
         def clear(b):
             kvx[b] = jnp.zeros((128, 128), BF16)
-        loop(g + 1, GRP, clear)
+        loop(g + 1, 4 * zh + 4, clear)
         arrived(f_in, f_rs)
         i, j = iota((128, TOK), 0), iota((128, TOK), 1)
         base = 16 * (i // 4) + i % 4
+        keys = onehot(j == base)
         rows = f_in[...].reshape(TOK, 128)
-        kvx[g] = nn(onehot(j == base), rows).astype(BF16)
+        kvx[g] = nn(keys, rows).astype(BF16)
         qz[...] = nn(onehot(j == base + 4), rows).astype(BF16)
-        pl.semaphore_wait(barrier, 6 - zh)
-        loop(zh + 1, 4, lambda z: to_z(z).start())
-        loop(gx + 1, 4, lambda x: to_x(g, x_ss.at[x], x).start())
-
-        def step(z):
+
+        @pl.when(zh > 1)
+        def _():
+            pl.semaphore_wait(go, 1)
+        for i in range(1, 4):
+            @pl.when(gx + i < 4)
+            def _():
+                on_x(g, i).start()
+
+        @pl.when(zh < 2)
+        def _():
+            pl.semaphore_wait(barrier, 2)
+            for i in range(2):
+                on_z(i).start()
+
+        @pl.when(zh == 3)
+        def _():
+            arrived(g_in, g_rs)
+            kvx[g - 4] = nn(keys, g_in[...].reshape(TOK, 128)).astype(BF16)
+            for i in range(1, 4):
+                on_x(g - 4, i).start()
+
+        def passing(z):
             b = 4 * z + gx
             arrived(kvx.at[b], blk_rs.at[b])
+
+            @pl.when(zh == 1)
+            def _():
+                on_z_pass().start()
             for i in range(1, 4):
-                to_x(b, fw_ss.at[z, i - 1], (gx + i) % 4).start()
-        loop(0, zh, step)
+                on_x(b, i).start()
+        loop(0, jnp.minimum(zh, 2), passing)
 
     for h in range(HEADS):
         spread[h] = onehot(iota((128, TOK), 1) - 8 * (iota((128, TOK), 0) % 64) == off_ref[0, h])
@@ -323,32 +381,29 @@
 
     @pl.when(is_far)
     def _():
-        def step(b):
-            @pl.when(b % 4 != gx)
-            def _():
-                arrived(kvx.at[b], blk_rs.at[b])
-        loop(0, g, step)
         qf = qz[...]
-        limit = iota((TOK, 128), 1) + 128 * g
-        row = iota((TOK, 128), 0)
-
-        def part(b):
-            return kvx[4 * b:4 * b + 4].reshape(TOK, 128)
-
-        m = None
-        xs = []
-        for b in range(4):
-            x = nt(part(b), qf)
-            x = jnp.where(row + TOK * b <= limit, x, NEG)
-            xs.append(x)
-            y = jnp.max(x, axis=0, keepdims=True)
-            m = y if m is None else jnp.maximum(m, y)
-        o = None
-        for b in range(4):
-            xt = nt(eye, part(b))
-            xt = jnp.where(row_v, 1.0, xt).astype(BF16)
-            y = nn(xt, jnp.exp2((xs[b] - m) * C).astype(BF16))
-            o = y if o is None else o + y
+        limit = iota((TOK, 128), 1) - iota((TOK, 128), 0)
+        far_m[...] = jnp.full((1, 128), NEG, F32)
+        far_o[...] = jnp.zeros((128, 128), F32)
+
+        def slab(n):
+            z = jnp.where((zh == 3) & (n > 1), 5 - n, n)
+
+            def wait(b):
+                @pl.when(b % 4 != gx)
+                def _():
+                    arrived(kvx.at[b], blk_rs.at[b])
+            loop(4 * z, jnp.minimum(4 * z + 4, g), wait)
+            part = kvx[pl.ds(4 * z, 4)].reshape(TOK, 128)
+            x = jnp.where(limit >= TOK * z - 128 * g, nt(part, qf), NEG)
+            old = far_m[...]
+            new = jnp.maximum(old, jnp.max(x, axis=0, keepdims=True))
+            xt = jnp.where(row_v, 1.0, nt(eye, part)).astype(BF16)
+            y = nn(xt, jnp.exp2((x - new) * C).astype(BF16))
+            far_o[...] = far_o[...] * jnp.exp2((old - new) * C) + y
+            far_m[...] = new
+        loop(0, zh + 1, slab)
+        m, o = far_m[...], far_o[...]
         total = o[0:1]
         norm = (o[64:128] / total).astype(BF16)
         ls = three(m * C + jnp.log(total) * math.log2(math.e))
@@ -369,21 +424,30 @@
         left = jnp.concatenate([jnp.where(low48, x, zero), jnp.where(low, zero, x[0:32])], axis=0)
         u = nn(left, spread[h])
         l1 = jnp.where(tok % 8 == off_ref[0, h], u[32:33] + u[33:34] + u[34:35], NEG)
+        m0 = top[h]
+        big = jnp.maximum(m0, l1)
+        w0, w1 = jnp.exp2(m0 - big), jnp.exp2(l1 - big)
+        top[h] = big
+        tot[h] = w0 * tot[h] + w1
+        for a in range(2):
+            rows = slice(64 * h + 32 * a, 64 * h + 32 * a + 32)
+            acc[rows, :] = acc[rows, :] * w0 + u[48 * a:48 * a + 32] * w1
+    for h in range(HEADS):
         arrived(fret_in.at[h], fret_rs.at[h])
         w = tn(fret_in[h], far_hot[h])
         l2 = jnp.where(tok % 128 == off_ref[1, h], w[64:65] + w[65:66] + w[66:67], NEG)
         m0 = top[h]
-        big = jnp.maximum(jnp.maximum(m0, l1), l2)
-        w0, w1, w2 = jnp.exp2(m0 - big), jnp.exp2(l1 - big), jnp.exp2(l2 - big)
-        inv = 1.0 / (w0 * tot[h] + w1 + w2)
-        w0, w1, w2 = w0 * inv, w1 * inv, w2 * inv
-        for a in range(2):
-            rows = slice(64 * h + 32 * a, 64 * h + 32 * a + 32)
-            n1 = u[48 * a:48 * a + 32]
-            n2 = w[32 * a:32 * a + 32]
-            out_ref[rows, :] = (acc[rows, :] * w0 + n1 * w1 + n2 * w2).astype(BF16)
+        big = jnp.maximum(m0, l2)
+        w0, w2 = jnp.exp2(m0 - big), jnp.exp2(l2 - big)
+        inv = 1.0 / (w0 * tot[h] + w2)
+        rows = slice(64 * h, 64 * h + 64)
+        out_ref[rows, :] = (acc[rows, :] * (w0 * inv) + w[0:64] * (w2 * inv)).astype(BF16)
 
     sent(n_send.at[:, pl.ds(0, 64)], out_ss.at[2])
+
+    @pl.when(zh == 2)
+    def _():
+        sent(f_send, out_ss.at[3])
 
     @pl.when(is_near)
     def _():
@@ -398,13 +462,21 @@
     def _():
         sent(f_send.at[pl.ds(0, HEADS - 1)], out_ss.at[0])
         sent(fret_send.at[pl.ds(0, SEQ - 1)], ret_ss.at[1])
-        loop(gx + 1, 4, lambda x: to_x(g, x_ss.at[x], x).wait_send())
-        loop(zh + 1, 4, lambda z: to_z(z).wait_send())
-
-        def step(z):
-            for i in range(1, 4):
-                to_x(4 * z + gx, fw_ss.at[z, i - 1], (gx + i) % 4).wait_send()
-        loop(0, zh, step)
+        for i in range(1, 4):
+            @pl.when(gx + i < 4)
+            def _():
+                on_x(g, i).wait_send()
+
+            loop(0, zh, lambda z: on_x(4 * z + gx, i).wait_send())
+
+        @pl.when(zh < 2)
+        def _():
+            for i in range(2):
+                on_z(i).wait_send()
+
+        @pl.when(zh == 1)
+        def _():
+            on_z_pass().wait_send()
 
     @pl.when(jnp.logical_not(is_far))
     def _():
@@ -430,6 +502,7 @@
             vm((16, 96, 128), BF16),
             vm((16, 64, 128), BF16),
             vm((SEQ, 16, 128), BF16),
+            vm((SEQ, 16, 128), BF16),
             vm((128, 128), BF16),
             vm((8, 128, 256), BF16),
             vm((8, 256, 256), F32),
@@ -443,13 +516,15 @@
             vm((HEADS, 1, TOK), F32),
             vm((HEADS, 128, TOK), BF16),
             vm((HEADS, 16, TOK), BF16),
-            dma((4,)), dma((3,)), dma((4,)), dma((4,)), dma,
-            dma((4,)), dma((4,)), dma((3, 3)), dma((GRP,)),
+            vm((1, 128), F32),
+            vm((128, 128), F32),
+            dma((4,)), dma((4,)), dma((4,)), dma((4,)), dma, dma,
+            dma((3,)), dma((4, 3)), dma((GRP,)),
             pltpu.SemaphoreType.REGULAR,
             dma((2,)), dma((HEADS,)), dma((HEADS,)),
         ],
         compiler_params=pltpu.CompilerParams(
-            collective_id=0, has_side_effects=True, vmem_limit_bytes=56 * 1024 * 1024
+            collective_id=0, has_side_effects=True, vmem_limit_bytes=55783424
         ),
     )(queries, keys, values, offsets)
     return tn(merged, out_weight).astype(BF16)

time: 35.4 us -> 34.1 us (0.963)
  Pallas kernels: 32.8 us -> 31.7 us
  matrix products: 2.47 us -> 1.48 us
  local copies, waits for them, and re-layouts: 0.01 us -> 0.75 us
    pallas_call x1, Pallas kernels: 32.8 us -> 31.7 us  [on_device(): pl.pallas_call(kernel, out_shape=jax.ShapeDtypeStruct((HEADS * HD, TOK),...]
    dot_general x1, matrix products: 2.47 us -> 1.48 us  [tn(): lax.dot_general(a, b, (((0,), (0,)), ((), ())), preferred_element_type=F32)]
    unnamed x2 -> x4, local copies, waits for them, and re-layouts: 0.01 us -> 0.75 us
where the time goes in v3:
time: 34.1 us; the launch traced here: 33.9 us
  Pallas kernels  31.7 us (93%)
  matrix products  1.48 us (4%)
  local copies, waits for them, and re-layouts  0.75 us (2%)
    pallas_call x1, Pallas kernels, on_device(): pl.pallas_call(kernel, out_shape=jax.ShapeDtypeStruct((HEADS * HD, TOK),...  31.7 us
    dot_general x1, matrix products, tn(): lax.dot_general(a, b, (((0,), (0,)), ((), ())), preferred_element_type=F32)  1.48 us
    unnamed x4, local copies, waits for them, and re-layouts  0.75 us

profile of v3, /device:TPU:385, one launch (start us, length us, event | category | flops | bytes accessed | tf_op | source)
XLA Modules:
  0.0 33.9 jit_solution(9768390366017678386)
XLA Ops:
  0.0 0.0 copy-start
  0.0 0.0 copy-start.1
  0.0 0.7 %copy-done.1 = s32[2,6]{1,0:T(2,128)S(1)} copy-done((s32[2,6]{1,0:T(2,128)S(1)}, s32[2,6]{1,0:T(2,128)}, u32[]{:S(2)}) %copy-start.1) | copy-done | bytes 72
  0.7 31.7 %shard_map.55 = bf16[384,512]{1,0:T(8,128)(2,1)S(1)} custom-call(bf16[512,384]{1,0:T(8,128)(2,1)} %q_hbm.1, bf16[512,384]{1,0:T(8,128)(2,1)} %k_hbm.1, bf16[512,384]{1,0:T(8,128)(2,1)} %v_hbm.1, s32[2,6]{1,0:T(2,128)S(1)} %copy-done.1), custom_call_target="tpu_custom_call" | custom-call | tf_op jit(solution)/shard_map/pallas_call | solution.py:490
  32.5 0.0 copy-done
  32.5 1.5 %convolution_convert_fusion = bf16[512,768]{1,0:T(8,128)(2,1)} fusion(bf16[384,512]{1,0:T(8,128)(2,1)S(1)} %shard_map.55, bf16[384,768]{1,0:T(8,128)(2,1)S(1)} %copy-done), kind=kOutput, calls=%fused_computation | convolution fusion | flops 302383104 | bytes 1769472 | tf_op jit(solution)/shard_map/dot_general | solution.py:31
Async XLA Ops:
  0.0 32.5 %copy-start = (bf16[384,768]{1,0:T(8,128)(2,1)S(1)}, bf16[384,768]{1,0:T(8,128)(2,1)}, u32[]{:S(2)}) copy-start(bf16[384,768]{1,0:T(8,128)(2,1)} %param.9) | copy-start | bytes 1769476
  0.0 0.7 %copy-start.1 = (s32[2,6]{1,0:T(2,128)S(1)}, s32[2,6]{1,0:T(2,128)}, u32[]{:S(2)}) copy-start(s32[2,6]{1,0:T(2,128)} %off_hbm.1) | copy-start | bytes 148

commit v4 on v3

--- a/solution.py
+++ b/solution.py
@@ -102,6 +102,26 @@
     def hello(axis, target):
         pl.semaphore_signal(barrier, inc=1, device_id={axis: target}, device_id_type=MESH)
 
+    @pl.when(is_far)
+    def _():
+        for i in range(1, 4):
+            pl.semaphore_signal(
+                barrier, inc=1, device_id={"grp": 4 * zh + (gx + i) % 4, "seq": sibling}, device_id_type=MESH
+            )
+
+        @pl.when((zh == 1) | (zh == 2))
+        def _():
+            hello("grp", g - 4)
+
+        @pl.when(zh == 3)
+        def _():
+            hello("grp", g - 12)
+            hello("grp", g - 8)
+
+            loop(0, SEQ, lambda i: pl.semaphore_signal(
+                barrier, inc=1, device_id={"grp": g - 4, "seq": i}, device_id_type=MESH
+            ))
+
     @pl.when(is_near | is_far)
     def _():
         def step(i):
@@ -109,26 +129,6 @@
             def _():
                 hello("seq", i)
         loop(0, SEQ, step)
-
-    @pl.when(is_far)
-    def _():
-        for i in range(1, 4):
-            pl.semaphore_signal(
-                barrier, inc=1, device_id={"grp": 4 * zh + (gx + i) % 4, "seq": sibling}, device_id_type=MESH
-            )
-
-        @pl.when((zh == 1) | (zh == 2))
-        def _():
-            hello("grp", g - 4)
-
-        @pl.when(zh == 3)
-        def _():
-            hello("grp", g - 12)
-            hello("grp", g - 8)
-
-            loop(0, SEQ, lambda i: pl.semaphore_signal(
-                barrier, inc=1, device_id={"grp": g - 4, "seq": i}, device_id_type=MESH
-            ))
 
     low = iota((32, 128), 1) < HD
     low16 = iota((16, 128), 1) < HD
@@ -387,7 +387,7 @@
         far_o[...] = jnp.zeros((128, 128), F32)
 
         def slab(n):
-            z = jnp.where((zh == 3) & (n > 1), 5 - n, n)
+            z = jnp.where(zh > 1, jnp.where(n == 0, 0, zh - n + 1), zh - n)
 
             def wait(b):
                 @pl.when(b % 4 != gx)

time: 34.1 us -> 33 us (0.968)
  Pallas kernels: 31.7 us -> 30.6 us
    pallas_call x1, Pallas kernels: 31.7 us -> 30.6 us  [on_device(): pl.pallas_call(kernel, out_shape=jax.ShapeDtypeStruct((HEADS * HD, TOK),...]
where the time goes in v4:
time: 33 us; the launch traced here: 32.8 us
  Pallas kernels  30.6 us (93%)
  matrix products  1.48 us (4%)
  local copies, waits for them, and re-layouts  0.75 us (2%)
    pallas_call x1, Pallas kernels, on_device(): pl.pallas_call(kernel, out_shape=jax.ShapeDtypeStruct((HEADS * HD, TOK),...  30.6 us
    dot_general x1, matrix products, tn(): lax.dot_general(a, b, (((0,), (0,)), ((), ())), preferred_element_type=F32)  1.48 us
    unnamed x4, local copies, waits for them, and re-layouts  0.75 us

profile of v4, /device:TPU:385, one launch (start us, length us, event | category | flops | bytes accessed | tf_op | source)
XLA Modules:
  0.0 32.8 jit_solution(5807749052251255014)
XLA Ops:
  0.0 0.0 copy-start
  0.0 0.0 copy-start.1
  0.0 0.7 %copy-done.1 = s32[2,6]{1,0:T(2,128)S(1)} copy-done((s32[2,6]{1,0:T(2,128)S(1)}, s32[2,6]{1,0:T(2,128)}, u32[]{:S(2)}) %copy-start.1) | copy-done | bytes 72
  0.7 30.6 %shard_map.55 = bf16[384,512]{1,0:T(8,128)(2,1)S(1)} custom-call(bf16[512,384]{1,0:T(8,128)(2,1)} %q_hbm.1, bf16[512,384]{1,0:T(8,128)(2,1)} %k_hbm.1, bf16[512,384]{1,0:T(8,128)(2,1)} %v_hbm.1, s32[2,6]{1,0:T(2,128)S(1)} %copy-done.1), custom_call_target="tpu_custom_call" | custom-call | tf_op jit(solution)/shard_map/pallas_call | solution.py:490
  31.3 0.0 copy-done
  31.3 1.5 %convolution_convert_fusion = bf16[512,768]{1,0:T(8,128)(2,1)} fusion(bf16[384,512]{1,0:T(8,128)(2,1)S(1)} %shard_map.55, bf16[384,768]{1,0:T(8,128)(2,1)S(1)} %copy-done), kind=kOutput, calls=%fused_computation | convolution fusion | flops 302383104 | bytes 1769472 | tf_op jit(solution)/shard_map/dot_general | solution.py:31
Async XLA Ops:
  0.0 31.3 %copy-start = (bf16[384,768]{1,0:T(8,128)(2,1)S(1)}, bf16[384,768]{1,0:T(8,128)(2,1)}, u32[]{:S(2)}) copy-start(bf16[384,768]{1,0:T(8,128)(2,1)} %param.9) | copy-start | bytes 1769476
  0.0 0.7 %copy-start.1 = (s32[2,6]{1,0:T(2,128)S(1)}, s32[2,6]{1,0:T(2,128)}, u32[]{:S(2)}) copy-start(s32[2,6]{1,0:T(2,128)} %off_hbm.1) | copy-start | bytes 148

commit v5 on v4

--- a/solution.py
+++ b/solution.py
@@ -70,7 +70,7 @@
     q_hbm, k_hbm, v_hbm, off_hbm, out_ref,
     q_ref, k_ref, v_ref, off_ref,
     n_send, f_send, n_in, o_in, f_in, g_in, qz, kvt, scr, ret_send, ret_in,
-    kvx, fret_send, fret_in, acc, top, tot, spread, far_hot, far_m, far_o,
+    kvx, fret_send, fret_in, acc, top, tot, spread, far_hot, far_m, far_o, place,
     in_sem, out_ss, n_rs, o_rs, f_rs, g_rs, z_ss, x_ss, blk_rs, go, ret_ss, ret_rs, fret_rs,
 ):
     s = lax.axis_index("seq")
@@ -304,7 +304,7 @@
         @pl.when(zh < 2)
         def _():
             pl.semaphore_wait(barrier, 2)
-            for i in range(2):
+            for i in (1, 0):
                 on_z(i).start()
 
         @pl.when(zh == 3)
@@ -381,6 +381,8 @@
 
     @pl.when(is_far)
     def _():
+        i, j = iota((TOK, 128), 0), iota((TOK, 128), 1)
+        place[...] = onehot((j == 4 * (i // 16) + i % 16) & (i % 16 < 4))
         qf = qz[...]
         limit = iota((TOK, 128), 1) - iota((TOK, 128), 0)
         far_m[...] = jnp.full((1, 128), NEG, F32)
@@ -410,9 +412,7 @@
         r = iota((64, 128), 0)
         tail = jnp.where(r == 0, ls[0], jnp.where(r == 1, ls[1], jnp.where(r == 2, ls[2], 0.0)))
         both = jnp.concatenate([norm, tail.astype(BF16)], axis=0)
-        i, j = iota((TOK, 128), 0), iota((TOK, 128), 1)
-        place = onehot((j == 4 * (i // 16) + i % 16) & (i % 16 < 4))
-        fret_send[...] = nt(place, both).astype(BF16).reshape(SEQ, 16, 128)
+        fret_send[...] = nt(place[...], both).astype(BF16).reshape(SEQ, 16, 128)
         loop(0, SEQ, lambda i: send(fret_send.at[i], fret_in.at[head], ret_ss.at[1], fret_rs.at[head], i))
 
     tok = iota((1, TOK), 1)
@@ -518,6 +518,7 @@
             vm((HEADS, 16, TOK), BF16),
             vm((1, 128), F32),
             vm((128, 128), F32),
+            vm((TOK, 128), BF16),
             dma((4,)), dma((4,)), dma((4,)), dma((4,)), dma, dma,
             dma((3,)), dma((4, 3)), dma((GRP,)),
             pltpu.SemaphoreType.REGULAR,

time: 33 us -> 33 us (level)
  no operation moved by 1% of the time
where the time goes in v5:
time: 33 us; the launch traced here: 32.8 us
  Pallas kernels  30.6 us (93%)
  matrix products  1.48 us (4%)
  local copies, waits for them, and re-layouts  0.75 us (2%)
    pallas_call x1, Pallas kernels, on_device(): pl.pallas_call(kernel, out_shape=jax.ShapeDtypeStruct((HEADS * HD, TOK),...  30.6 us
    dot_general x1, matrix products, tn(): lax.dot_general(a, b, (((0,), (0,)), ((), ())), preferred_element_type=F32)  1.48 us
    unnamed x4, local copies, waits for them, and re-layouts  0.75 us

profile of v5, /device:TPU:385, one launch (start us, length us, event | category | flops | bytes accessed | tf_op | source)
XLA Modules:
  0.0 32.8 jit_solution(14185119591105239697)
XLA Ops:
  0.0 0.0 copy-start
  0.0 0.0 copy-start.1
  0.0 0.7 %copy-done.1 = s32[2,6]{1,0:T(2,128)S(1)} copy-done((s32[2,6]{1,0:T(2,128)S(1)}, s32[2,6]{1,0:T(2,128)}, u32[]{:S(2)}) %copy-start.1) | copy-done | bytes 72
  0.7 30.6 %shard_map.55 = bf16[384,512]{1,0:T(8,128)(2,1)S(1)} custom-call(bf16[512,384]{1,0:T(8,128)(2,1)} %q_hbm.1, bf16[512,384]{1,0:T(8,128)(2,1)} %k_hbm.1, bf16[512,384]{1,0:T(8,128)(2,1)} %v_hbm.1, s32[2,6]{1,0:T(2,128)S(1)} %copy-done.1), custom_call_target="tpu_custom_call" | custom-call | tf_op jit(solution)/shard_map/pallas_call | solution.py:490
  31.3 0.0 copy-done
  31.3 1.5 %convolution_convert_fusion = bf16[512,768]{1,0:T(8,128)(2,1)} fusion(bf16[384,512]{1,0:T(8,128)(2,1)S(1)} %shard_map.55, bf16[384,768]{1,0:T(8,128)(2,1)S(1)} %copy-done), kind=kOutput, calls=%fused_computation | convolution fusion | flops 302383104 | bytes 1769472 | tf_op jit(solution)/shard_map/dot_general | solution.py:31
Async XLA Ops:
  0.0 31.3 %copy-start = (bf16[384,768]{1,0:T(8,128)(2,1)S(1)}, bf16[384,768]{1,0:T(8,128)(2,1)}, u32[]{:S(2)}) copy-start(bf16[384,768]{1,0:T(8,128)(2,1)} %param.9) | copy-start | bytes 1769476
  0.0 0.7 %copy-start.1 = (s32[2,6]{1,0:T(2,128)S(1)}, s32[2,6]{1,0:T(2,128)}, u32[]{:S(2)}) copy-start(s32[2,6]{1,0:T(2,128)} %off_hbm.1) | copy-start | bytes 148

commit v6 on v4

--- a/solution.py
+++ b/solution.py
@@ -285,6 +285,20 @@
         def clear(b):
             kvx[b] = jnp.zeros((128, 128), BF16)
         loop(g + 1, 4 * zh + 4, clear)
+        def passing(z):
+            b = 4 * z + gx
+            arrived(kvx.at[b], blk_rs.at[b])
+
+            @pl.when(zh == 1)
+            def _():
+                on_z_pass().start()
+            for i in range(1, 4):
+                on_x(b, i).start()
+        @pl.when(zh == 3)
+        def _():
+            pl.semaphore_wait(go, 1)
+            passing(0)
+
         arrived(f_in, f_rs)
         i, j = iota((128, TOK), 0), iota((128, TOK), 1)
         base = 16 * (i // 4) + i % 4
@@ -293,7 +307,7 @@
         kvx[g] = nn(keys, rows).astype(BF16)
         qz[...] = nn(onehot(j == base + 4), rows).astype(BF16)
 
-        @pl.when(zh > 1)
+        @pl.when(zh == 2)
         def _():
             pl.semaphore_wait(go, 1)
         for i in range(1, 4):
@@ -314,16 +328,7 @@
             for i in range(1, 4):
                 on_x(g - 4, i).start()
 
-        def passing(z):
-            b = 4 * z + gx
-            arrived(kvx.at[b], blk_rs.at[b])
-
-            @pl.when(zh == 1)
-            def _():
-                on_z_pass().start()
-            for i in range(1, 4):
-                on_x(b, i).start()
-        loop(0, jnp.minimum(zh, 2), passing)
+        loop(jnp.where(zh == 3, 1, 0), jnp.minimum(zh, 2), passing)
 
     for h in range(HEADS):
         spread[h] = onehot(iota((128, TOK), 1) - 8 * (iota((128, TOK), 0) % 64) == off_ref[0, h])

time: 33 us -> 32.3 us (0.979)
  Pallas kernels: 30.6 us -> 29.9 us
    pallas_call x1, Pallas kernels: 30.6 us -> 29.9 us  [on_device(): pl.pallas_call(kernel, out_shape=jax.ShapeDtypeStruct((HEADS * HD, TOK),...]
where the time goes in v6:
time: 32.3 us; the launch traced here: 32.1 us
  Pallas kernels  29.9 us (93%)
  matrix products  1.48 us (5%)
  local copies, waits for them, and re-layouts  0.75 us (2%)
    pallas_call x1, Pallas kernels, on_device(): pl.pallas_call(kernel, out_shape=jax.ShapeDtypeStruct((HEADS * HD, TOK),...  29.9 us
    dot_general x1, matrix products, tn(): lax.dot_general(a, b, (((0,), (0,)), ((), ())), preferred_element_type=F32)  1.48 us
    unnamed x4, local copies, waits for them, and re-layouts  0.75 us

profile of v6, /device:TPU:385, one launch (start us, length us, event | category | flops | bytes accessed | tf_op | source)
XLA Modules:
  0.0 32.1 jit_solution(1428495515069145853)
XLA Ops:
  0.0 0.0 copy-start
  0.0 0.0 copy-start.1
  0.0 0.7 %copy-done.1 = s32[2,6]{1,0:T(2,128)S(1)} copy-done((s32[2,6]{1,0:T(2,128)S(1)}, s32[2,6]{1,0:T(2,128)}, u32[]{:S(2)}) %copy-start.1) | copy-done | bytes 72
  0.7 29.9 %shard_map.55 = bf16[384,512]{1,0:T(8,128)(2,1)S(1)} custom-call(bf16[512,384]{1,0:T(8,128)(2,1)} %q_hbm.1, bf16[512,384]{1,0:T(8,128)(2,1)} %k_hbm.1, bf16[512,384]{1,0:T(8,128)(2,1)} %v_hbm.1, s32[2,6]{1,0:T(2,128)S(1)} %copy-done.1), custom_call_target="tpu_custom_call" | custom-call | tf_op jit(solution)/shard_map/pallas_call | solution.py:495
  30.6 0.0 copy-done
  30.6 1.5 %convolution_convert_fusion = bf16[512,768]{1,0:T(8,128)(2,1)} fusion(bf16[384,512]{1,0:T(8,128)(2,1)S(1)} %shard_map.55, bf16[384,768]{1,0:T(8,128)(2,1)S(1)} %copy-done), kind=kOutput, calls=%fused_computation | convolution fusion | flops 302383104 | bytes 1769472 | tf_op jit(solution)/shard_map/dot_general | solution.py:31
Async XLA Ops:
  0.0 30.6 %copy-start = (bf16[384,768]{1,0:T(8,128)(2,1)S(1)}, bf16[384,768]{1,0:T(8,128)(2,1)}, u32[]{:S(2)}) copy-start(bf16[384,768]{1,0:T(8,128)(2,1)} %param.9) | copy-start | bytes 1769476
  0.0 0.7 %copy-start.1 = (s32[2,6]{1,0:T(2,128)S(1)}, s32[2,6]{1,0:T(2,128)}, u32[]{:S(2)}) copy-start(s32[2,6]{1,0:T(2,128)} %off_hbm.1) | copy-start | bytes 148
